TPU v7x, 32 devices: a whole 2x2x4 slice. The times are simulated.
32 devices in a mesh: seq: 8 (over y, x, core), head: 4 (over z).
Axes of the slice: x: 2, y: 2, z: 4, core: 2. Of those that a mesh axis runs over, the one named last changes fastest.
Arguments:
- queries: bfloat16 [2048, 3072], P('seq', 'head'), may hold values from -6 to 6
- keys: bfloat16 [2048, 3072], P('seq', 'head'), may hold values from -6 to 6
- values: bfloat16 [2048, 3072], P('seq', 'head'), may hold values from -6 to 6
- grad_out: bfloat16 [2048, 3072], P('seq', 'head'), may hold values from -6 to 6
- scene_keys: bfloat16 [32, 3072], P(('seq', 'head')), may hold values from -6 to 6
- scene_values: bfloat16 [32, 3072], P(('seq', 'head')), may hold values from -6 to 6
- valid: int32 [32], replicated, may hold values from 2 to 64
- pattern: int32 [32, 3], replicated, may hold values from 0 to 31, as said below
Outputs:
- attended: bfloat16 [2048, 3072], P('seq', 'head')
- grad_queries: bfloat16 [2048, 3072], P('seq', 'head')
- grad_keys: bfloat16 [2048, 3072], P('seq', 'head')
- grad_values: bfloat16 [2048, 3072], P('seq', 'head')
- grad_scene_keys: bfloat16 [32, 3072], P(('seq', 'head'))
- grad_scene_values: bfloat16 [32, 3072], P(('seq', 'head'))
Inputs may be any that keep to these rules, and one draw needn't show every extreme that they name: `pattern`: the 12 entries of the query blocks of one seq index all name blocks of other seq indices; no seq index supplies more than 2 of them to one seq index, and to each seq index some seq index supplies exactly 2.
All inputs are finite; a program needn't handle non-finite values.
Results may differ from a plain program's by a relative error of at most 0.0061.
Values may be sent and summed in bfloat16 or wider, within the bound.
A program may use at most 128 MiB of HBM per device.

v0:
```python
import jax
import jax.numpy as jnp
from jax import lax
from jax.sharding import PartitionSpec as P

DH = 128
BLK = 64
RAND = 3


def extended_2(block, sides, width):
    for axis, dim in sides:
        count = lax.axis_size(axis)
        forward = [(i, i + 1) for i in range(count - 1)]
        backward = [(target, source) for source, target in forward]
        low = lax.ppermute(
            lax.slice_in_dim(block, block.shape[dim] - width, None, axis=dim), axis, forward
        )
        high = lax.ppermute(lax.slice_in_dim(block, 0, width, axis=dim), axis, backward)
        block = jnp.concatenate([low, block, high], axis=dim)
    return block


def passed_along(x, axis, by):
    length = lax.axis_size(axis)
    pairs = [(i, i + by) for i in range(length) if 0 <= i + by < length]
    return lax.ppermute(x, axis, pairs)


def block_terms(query, all_keys, all_values, key_live, query_live, grad_out):
    scale = DH ** (-0.5)
    scores = (
        jnp.einsum("gqhd,gkhd->ghqk", query, all_keys, preferred_element_type=jnp.float32) * scale
    )
    scores = jnp.where(key_live[:, None, None, :], scores, -1e30)
    highest = jnp.max(scores, axis=3, keepdims=True)
    expo = jnp.exp(scores - highest)
    prob = expo / jnp.sum(expo, axis=3, keepdims=True)
    prob_round = prob.astype(jnp.bfloat16)
    live_rows = query_live[:, :, None, None]
    attended = jnp.einsum(
        "ghqk,gkhd->gqhd", prob_round, all_values, preferred_element_type=jnp.float32
    )
    attended = jnp.where(live_rows, attended, 0.0).astype(jnp.bfloat16)
    grad_live = jnp.where(live_rows, grad_out, 0.0)
    dprob = jnp.einsum("gqhd,gkhd->ghqk", grad_live, all_values, preferred_element_type=jnp.float32)
    delta = jnp.sum(prob * dprob, axis=3, keepdims=True)
    dscore = (prob * (dprob - delta) * scale).astype(jnp.bfloat16)
    grad_query = jnp.einsum("ghqk,gkhd->gqhd", dscore, all_keys, preferred_element_type=jnp.float32)
    grad_k = jnp.einsum("ghqk,gqhd->gkhd", dscore, query, preferred_element_type=jnp.float32)
    grad_v = jnp.einsum(
        "ghqk,gqhd->gkhd", prob_round, grad_live, preferred_element_type=jnp.float32
    )
    return (attended, grad_query.astype(jnp.bfloat16), grad_k, grad_v)


def per_device(queries, keys, values, grad_out, scene_keys, scene_values, valid, pattern):
    seq_count = lax.axis_size("seq")
    position = lax.axis_index("seq")
    features = queries.shape[1]
    head_count = features // DH
    blocks_dev = queries.shape[0] // BLK
    group_size = min(8, blocks_dev)
    requests = blocks_dev * RAND
    slot_count = (requests + seq_count - 2) // (seq_count - 1)
    offsets = jnp.arange(BLK, dtype=jnp.int32)
    near_count = (3 + RAND) * BLK
    parted = (
        lax.all_to_all(scene_keys, "head", split_axis=1, concat_axis=0, tiled=True),
        lax.all_to_all(scene_values, "head", split_axis=1, concat_axis=0, tiled=True),
    )
    scene_k, scene_v = (
        lax.all_gather(parted[0], "seq", axis=0, tiled=True),
        lax.all_gather(parted[1], "seq", axis=0, tiled=True),
    )
    scene_rows_all = scene_k.shape[0]
    scene_kv = jnp.stack([scene_k, scene_v]).reshape(2, 1, scene_rows_all, head_count, DH)
    scene_kv = jnp.broadcast_to(scene_kv, (2, group_size, scene_rows_all, head_count, DH))
    stacked = jnp.stack([keys, values])
    extended = extended_2(stacked, (("seq", 1),), BLK)
    all_requests = pattern.reshape(seq_count, requests)
    source = all_requests // blocks_dev
    local_block = all_requests % blocks_dev
    from_here = source == position
    send_rank = jnp.cumsum(from_here.astype(jnp.int32), axis=1) - 1
    slot_ids = jnp.arange(slot_count, dtype=jnp.int32)
    marked = from_here[:, :, None] & (send_rank[:, :, None] == slot_ids[None, None, :])
    chosen = jnp.sum(jnp.where(marked, local_block[:, :, None], 0), axis=1)
    block_view = stacked.reshape(2, blocks_dev, BLK, features)
    outgoing = block_view[:, chosen]
    incoming = lax.all_to_all(outgoing, "seq", split_axis=1, concat_axis=1, tiled=True)
    own_requests = lax.dynamic_slice_in_dim(pattern, position * blocks_dev, blocks_dev, 0).reshape(
        requests
    )
    own_source = own_requests // blocks_dev
    earlier = jnp.tril(jnp.ones((requests, requests), jnp.bool_), -1)
    same_source = own_source[:, None] == own_source[None, :]
    recv_rank = jnp.sum((same_source & earlier).astype(jnp.int32), axis=1)
    recv_place = own_source * slot_count + recv_rank
    far_blocks = incoming.reshape(2, seq_count * slot_count, BLK, features)[:, recv_place]
    far_blocks = far_blocks.reshape(2, blocks_dev, RAND, BLK, features)
    padded_valid = jnp.concatenate([jnp.zeros((1,), jnp.int32), valid, jnp.zeros((1,), jnp.int32)])
    window_count = lax.dynamic_slice_in_dim(padded_valid, position * blocks_dev, blocks_dev + 2, 0)
    far_count = valid[own_requests].reshape(blocks_dev, RAND)
    query_count = lax.dynamic_slice_in_dim(valid, position * blocks_dev, blocks_dev, 0)
    scene_live = jnp.ones((group_size, scene_rows_all), jnp.bool_)
    ext_grad = jnp.zeros((2, blocks_dev + 2, BLK, features), jnp.float32)
    query_grp = queries.reshape(group_size, BLK, head_count, DH)
    grad_grp = grad_out.reshape(group_size, BLK, head_count, DH)
    window = extended.reshape(2, group_size + 2, BLK, features)
    near_kv = jnp.concatenate(
        [
            window[:, 0:group_size, None],
            window[:, 1 : group_size + 1, None],
            window[:, 2:, None],
            far_blocks,
        ],
        axis=2,
    )
    near_kv = near_kv.reshape(2, group_size, near_count, head_count, DH)
    joined_kv = jnp.concatenate([near_kv, scene_kv], axis=2)
    counts = jnp.concatenate(
        [
            window_count[0:group_size, None],
            window_count[1 : group_size + 1, None],
            window_count[2 : group_size + 2, None],
            far_count,
        ],
        axis=1,
    )
    near_live = (offsets[None, None, :] < counts[:, :, None]).reshape(group_size, near_count)
    key_live = jnp.concatenate([near_live, scene_live], axis=1)
    query_live = offsets[None, :] < query_count[0:group_size, None]
    attended, grad_query, grad_k, grad_v = block_terms(
        query_grp, joined_kv[0], joined_kv[1], key_live, query_live, grad_grp
    )
    both_grad = jnp.stack([grad_k, grad_v])
    near_grad = both_grad[:, :, :near_count].reshape(2, group_size, 3 + RAND, BLK, features)
    scene_grad = jnp.sum(both_grad[:, :, near_count:], axis=1)
    ext_grad = ext_grad.at[:, 0:group_size].add(near_grad[:, :, 0])
    ext_grad = ext_grad.at[:, 1 : group_size + 1].add(near_grad[:, :, 1])
    ext_grad = ext_grad.at[:, 2 : group_size + 2].add(near_grad[:, :, 2])
    random_parts = near_grad[:, :, 3:].astype(jnp.bfloat16)
    attended_parts = attended.reshape(group_size * BLK, features)
    query_parts = grad_query.reshape(group_size * BLK, features)
    random_terms = random_parts.reshape(2, requests, BLK, features)
    outgoing_grad = (
        jnp.zeros((2, seq_count * slot_count, BLK, features), jnp.bfloat16)
        .at[:, recv_place]
        .set(random_terms)
    )
    outgoing_grad = outgoing_grad.reshape(2, seq_count, slot_count, BLK, features)
    returned = lax.all_to_all(outgoing_grad, "seq", split_axis=1, concat_axis=1, tiled=True)
    selector = (
        chosen.reshape(-1)[:, None] == jnp.arange(blocks_dev, dtype=jnp.int32)[None, :]
    ).astype(jnp.bfloat16)
    gathered_grad = jnp.einsum(
        "sb,xsk->xbk",
        selector,
        returned.reshape(2, seq_count * slot_count, BLK * features),
        preferred_element_type=jnp.float32,
    )
    from_right = passed_along(ext_grad[:, 0].astype(jnp.bfloat16), "seq", -1).astype(jnp.float32)
    from_left = passed_along(ext_grad[:, blocks_dev + 1].astype(jnp.bfloat16), "seq", 1).astype(
        jnp.float32
    )
    inner = ext_grad[:, 1 : blocks_dev + 1]
    inner = inner.at[:, blocks_dev - 1].add(from_right).at[:, 0].add(from_left)
    total_grad = inner.reshape(2, blocks_dev, BLK * features) + gathered_grad
    grad_keys = total_grad[0].reshape(blocks_dev * BLK, features).astype(jnp.bfloat16)
    grad_values = total_grad[1].reshape(blocks_dev * BLK, features).astype(jnp.bfloat16)
    scene_terms_k = scene_grad[0].reshape(scene_rows_all, features)
    scene_terms_v = scene_grad[1].reshape(scene_rows_all, features)
    mine_k, mine_v = (
        lax.psum_scatter(scene_terms_k, "seq", scatter_dimension=0, tiled=True),
        lax.psum_scatter(scene_terms_v, "seq", scatter_dimension=0, tiled=True),
    )
    back_k, back_v = (
        lax.all_to_all(mine_k, "head", split_axis=0, concat_axis=1, tiled=True),
        lax.all_to_all(mine_v, "head", split_axis=0, concat_axis=1, tiled=True),
    )
    return (
        attended_parts,
        query_parts,
        grad_keys,
        grad_values,
        back_k.astype(jnp.bfloat16),
        back_v.astype(jnp.bfloat16),
    )


def solution(mesh):
    placed = (
        P("seq", "head"),
        P("seq", "head"),
        P("seq", "head"),
        P("seq", "head"),
        P(("seq", "head"), None),
        P(("seq", "head"), None),
        P(),
        P(),
    )
    return jax.shard_map(
        per_device,
        mesh=mesh,
        in_specs=placed,
        out_specs=(
            P("seq", "head"),
            P("seq", "head"),
            P("seq", "head"),
            P("seq", "head"),
            P(("seq", "head"), None),
            P(("seq", "head"), None),
        ),
        check_vma=False,
    )
```

profile of v0, /device:TPU:1, one launch (start us, length us, event | category | flops | bytes accessed | tf_op | source)
XLA Modules:
  0.0 310.6 jit_solution(7357923241083098513)
XLA Ops:
  3.2 5.4 %all-to-all-start.2 = ((bf16[4,2,384]{2,1,0:T(2,128)(2,1)}), bf16[4,2,384]{2,1,0:T(2,128)(2,1)S(1)}, u32[]{:S(2)}, u32[]{:S(2)}) async-start(bf16[4,2,384]{2,1,0:T(2,128)(2,1)} %reshape.647), calls=%async_computation.2 | async-start | bytes 12288 | tf_op jit(solution)/shard_map/all_to_all | solution.py:70
  13.2 4.5 %all-to-all-start.1 = ((bf16[4,2,384]{2,1,0:T(2,128)(2,1)}), bf16[4,2,384]{2,1,0:T(2,128)(2,1)S(1)}, u32[]{:S(2)}, u32[]{:S(2)}) async-start(bf16[4,2,384]{2,1,0:T(2,128)(2,1)} %reshape.649), calls=%async_computation.1 | async-start | bytes 12288 | tf_op jit(solution)/shard_map/all_to_all | solution.py:69
  20.2 3.9 %copy.154 = bf16[2,8,2,64,768]{4,3,2,0,1:T(8,128)(2,1)} copy(bf16[2,8,2,64,768]{4,3,0,2,1:T(8,128)(2,1)} %bitcast.155) | data formatting | bytes 6291456 | tf_op jit(solution)/shard_map/gather | solution.py:90
  24.6 5.2 %all-to-all-start = ((bf16[2,8,2,64,768]{4,3,2,0,1:T(8,128)(2,1)}), bf16[2,8,2,64,768]{4,3,2,0,1:T(8,128)(2,1)S(1)}, u32[]{:S(2)}, u32[]{:S(2)}) async-start(bf16[2,8,2,64,768]{4,3,2,0,1:T(8,128)(2,1)} %copy.154), calls=%async_computation | async-start | bytes 6291456 | tf_op jit(solution)/shard_map/all_to_all | solution.py:91
  31.6 3.5 %collective-permute-start = (bf16[2,64,768]{2,1,0:T(8,128)(2,1)}, bf16[2,64,768]{2,1,0:T(8,128)(2,1)}, u32[]{:S(2)}, u32[]{:S(2)}) collective-permute-start(bf16[2,64,768]{2,1,0:T(8,128)(2,1)} %get-tuple-element.79), channel_id=1, source_target_pairs={{0,4},{4,8},{8,12},{12,16},{16,20},{20,24},{24,28},{1,5},{5,9},{9,... | collective-permute-start | bytes 589832 | tf_op jit(solution)/shard_map/ppermute | solution.py:16
  63.4 11.6 %all-gather = bf16[1,32,768]{2,0,1:T(2,128)(2,1)} all-gather(bf16[1,4,768]{2,0,1:T(2,128)(2,1)S(1)} %bitcast.175), channel_id=2, replica_groups=mesh['seq'=8,'head'=4] {'seq'}, dimensions={1}, use_global_device_ids=true | all-gather | bytes 55296 | tf_op jit(solution)/shard_map/all_gather | solution.py:73
  79.0 10.4 %all-gather.1 = bf16[1,32,768]{2,0,1:T(2,128)(2,1)} all-gather(bf16[1,4,768]{2,0,1:T(2,128)(2,1)S(1)} %bitcast.176), channel_id=3, replica_groups=mesh['seq'=8,'head'=4] {'seq'}, dimensions={1}, use_global_device_ids=true | all-gather | bytes 55296 | tf_op jit(solution)/shard_map/all_gather | solution.py:74
  101.8 3.6 %pad_maximum_fusion = bf16[2,4,6,64,768]{4,3,2,1,0:T(8,128)(2,1)} fusion(bf16[2,4,1,64,768]{4,3,2,1,0:T(8,128)(2,1)} %get-tuple-element.75, bf16[2,4,1,64,768]{4,3,2,1,0:T(8,128)(2,1)} %get-tuple-element.76, bf16[2,4,1,64,768]{4,3,2,1,0:T(8,128)(2,1)S(1)} %copy-done.5, bf16[2,4,3,64,768]{4,3,0,2,1:T(8,128)(2,1)S(1)} %bitcast.159), kind=kLoop, calls=%fused_computation.15 | loop fusion | flops 18874368 | bytes 9437184 | tf_op jit(solution)/shard_map/concatenate | solution.py:111
  105.4 10.8 %reshape.587 = bf16[2,4,384,6,128]{4,3,2,1,0:T(8,128)(2,1)} reshape(bf16[2,4,6,64,768]{4,3,2,1,0:T(8,128)(2,1)} %pad_maximum_fusion) | data formatting | bytes 9437184 | tf_op jit(solution)/shard_map/reshape | solution.py:120
  116.1 4.1 %copy.162 = bf16[2,4,384,6,128]{4,2,3,1,0:T(8,128)(2,1)S(1)} copy(bf16[2,4,384,6,128]{4,3,2,1,0:T(8,128)(2,1)} %reshape.587) | data formatting | bytes 9437184 | tf_op jit(solution)/shard_map/reshape | solution.py:120
  127.0 3.7 %convolution_bitcast_fusion.1 = f32[1,4,416,6,128]{4,2,3,1,0:T(8,128)} fusion(bf16[4,64,6,128]{3,2,1,0:T(8,128)(2,1)S(1)} %copy-done.7, f32[4,6,64,416]{3,2,1,0:T(8,128)S(1)} %get-tuple-element.89, f32[4,6,64]{2,1,0:T(8,128)S(1)} %get-tuple-element.88), kind=kOutput, calls=%fused_computation.28 | convolution fusion | flops 164855808 | bytes 8067072 | tf_op jit(solution)/shard_map/ghqk,gqhd->gkhd/dot_general | solution.py:51
  130.7 14.9 %convolution_bitcast_fusion.2 = f32[1,4,416,6,128]{4,2,3,1,0:T(8,128)} fusion(f32[4,6,64,416]{3,2,1,0:T(8,128)S(1)} %fusion.39, bf16[4,64,6,128]{3,2,1,0:T(8,128)(2,1)} %reshape.589, f32[4,6,64,416]{3,2,1,0:T(8,128)} %copy-done.17, f32[4,6,64]{2,1,0:T(8,128)S(1)} %get-tuple-element.88), kind=kOutput, calls=%fused_computation.29 | convolution fusion | flops 168052640 | bytes 10622976 | tf_op jit(solution)/shard_map/ghqk,gqhd->gkhd/dot_general | solution.py:50
  149.9 3.9 %fusion.4 = f32[2,4,384,6,128]{4,2,3,1,0:T(8,128)} fusion(f32[1,4,416,6,128]{4,2,3,1,0:T(8,128)S(1)} %copy-done.3, f32[1,4,416,6,128]{4,2,3,1,0:T(8,128)S(1)} %copy-done.2), kind=kLoop, calls=%fused_computation.11 | loop fusion | flops 2359296 | bytes 19660800 | tf_op jit(solution)/shard_map/stack | solution.py:137
  155.3 23.6 %all-reduce.6 = (bf16[32,768]{1,0:T(8,128)(2,1)}, bf16[32,768]{1,0:T(8,128)(2,1)}) all-reduce(f32[32,768]{1,0:T(8,128)} %bitcast.174, f32[32,768]{1,0:T(8,128)} %bitcast.173), channel_id=4, replica_groups=mesh['seq'=8,'head'=4] {'seq'}, use_global_device_ids=true, to_apply=%region_8.9.clone | all-reduce | flops 49152 | bytes 294912
  180.8 4.8 %all-to-all-start.5 = ((bf16[4,2,384]{2,1,0:T(2,128)(2,1)}), bf16[4,2,384]{2,1,0:T(2,128)(2,1)}, u32[]{:S(2)}, u32[]{:S(2)}) async-start(bf16[4,2,384]{2,1,0:T(2,128)(2,1)} %reshape.653), calls=%async_computation.5 | async-start | bytes 12288 | tf_op jit(solution)/shard_map/all_to_all | solution.py:180
  190.0 3.5 %all-to-all-start.4 = ((bf16[4,2,384]{2,1,0:T(2,128)(2,1)}), bf16[4,2,384]{2,1,0:T(2,128)(2,1)S(1)}, u32[]{:S(2)}, u32[]{:S(2)}) async-start(bf16[4,2,384]{2,1,0:T(2,128)(2,1)} %reshape.651), calls=%async_computation.4 | async-start | bytes 12288 | tf_op jit(solution)/shard_map/all_to_all | solution.py:179
  193.5 12.9 %fusion.32 = bf16[4,64,6,128]{3,1,2,0:T(8,128)(2,1)} fusion(f32[4,6,64,416]{3,2,1,0:T(8,128)S(1)} %fusion.39, bf16[2,4,384,6,128]{4,2,3,1,0:T(8,128)(2,1)} %copy-done.1, bf16[2,4,32,6,128]{4,2,3,1,0:T(8,128)(2,1)S(1)} %broadcast_in_dim.108, f32[4,6,64,416]{3,2,1,0:T(8,128)} %copy-done.17, f32[4,6,64]{2,1,0:T(8,128)} %copy-done.18), kind=kOutput, calls=%fused_computation.46 | convolution fusion | flops 173361056 | bytes 18120704 | tf_op jit(solution)/shard_map/ghqk,gkhd->gqhd/dot_general | solution.py:49
  208.5 13.6 %copy.172 = f32[2,4,384,6,128]{4,3,2,1,0:T(8,128)} copy(f32[2,4,384,6,128]{4,2,3,1,0:T(8,128)} %fusion.4) | data formatting | bytes 18874368 | tf_op jit(solution)/shard_map/slice | solution.py:138
  222.0 12.5 %reshape.593 = f32[2,4,6,64,768]{4,3,2,1,0:T(8,128)} reshape(f32[2,4,384,6,128]{4,3,2,1,0:T(8,128)} %copy.172) | data formatting | bytes 18874368 | tf_op jit(solution)/shard_map/reshape | solution.py:138
  239.2 4.5 %scatter_fusion = bf16[2,16,64,768]{3,2,1,0:T(8,128)(2,1)S(1)} fusion(bf16[2,16,64,768]{3,2,1,0:T(8,128)(2,1)S(1)} %broadcast_in_dim.117, s32[12]{0:T(128)S(1)} %copy-done.12, bf16[12,2,64,768]{3,2,1,0:T(8,128)(2,1)} %copy.179), kind=kCustom, calls=%fused_computation.3 | custom fusion | bytes 7077936 | tf_op jit(solution)/shard_map/scatter | solution.py:150
  245.6 9.3 %all-to-all-start.3 = ((bf16[2,8,2,64,768]{4,3,2,0,1:T(8,128)(2,1)}), bf16[2,8,2,64,768]{4,3,2,0,1:T(8,128)(2,1)}, u32[]{:S(2)}, u32[]{:S(2)}) async-start(bf16[2,8,2,64,768]{4,3,2,0,1:T(8,128)(2,1)} %copy.180), calls=%async_computation.3 | async-start | bytes 6291456 | tf_op jit(solution)/shard_map/all_to_all | solution.py:153
  254.9 3.5 %fusion.35 = bf16[4,64,6,128]{3,1,2,0:T(8,128)(2,1)S(1)} fusion(bf16[2,4,32,6,128]{4,2,3,1,0:T(8,128)(2,1)S(1)} %broadcast_in_dim.108, bf16[2,4,384,6,128]{4,2,3,1,0:T(8,128)(2,1)} %copy-done.1, pred[4,64]{1,0:T(4,128)(4,1)S(1)} %copy-done.16, f32[4,6,64,416]{3,2,1,0:T(8,128)} %copy-done.17, f32[4,6,64]{2,1,0:T(8,128)S(1)} %copy-done.19), kind=kOutput, calls=%fused_computation.47 | convolution fusion | flops 170360832 | bytes 8067328 | tf_op jit(solution)/shard_map/ghqk,gkhd->gqhd/dot_general | solution.py:41
  269.3 26.2 %collective-permute-done.2 = bf16[2,64,768]{2,1,0:T(8,128)(2,1)} collective-permute-done((bf16[2,64,768]{2,1,0:T(8,128)(2,1)S(1)}, bf16[2,64,768]{2,1,0:T(8,128)(2,1)}, u32[]{:S(2)}, u32[]{:S(2)}) %collective-permute-start.2) | collective-permute-done | bytes 196640 | tf_op jit(solution)/shard_map/ppermute | solution.py:27
  304.5 3.7 %fusion.3 = bf16[2,4,49152]{2,1,0:T(4,128)(2,1)S(1)} fusion(bf16[2,16,49152]{2,1,0:T(8,128)(2,1)} %reshape.601, f32[2,4,49152]{2,0,1:T(2,128)} %reshape.642, s32[16]{0:T(128)S(1)} %copy-done.13), kind=kOutput, calls=%fused_computation.8 | convolution fusion | flops 13369408 | bytes 5505088 | tf_op jit(solution)/shard_map/sb,xsk->xbk/dot_general | solution.py:157
  (164 shorter events, 105.2 us)
Async XLA Ops:
  3.2 10.0 %all-to-all-start.2 = ((bf16[4,2,384]{2,1,0:T(2,128)(2,1)}), bf16[4,2,384]{2,1,0:T(2,128)(2,1)S(1)}, u32[]{:S(2)}, u32[]{:S(2)}) async-start(bf16[4,2,384]{2,1,0:T(2,128)(2,1)} %reshape.647), calls=%async_computation.2 | async-start | bytes 12288 | tf_op jit(solution)/shard_map/all_to_all | solution.py:70
  13.1 7.0 %copy-start.9 = (bf16[4,2,384]{2,1,0:T(2,128)(2,1)}, bf16[4,2,384]{2,1,0:T(2,128)(2,1)S(1)}, u32[]{:S(2)}) copy-start(bf16[4,2,384]{2,1,0:T(2,128)(2,1)S(1)} %all-to-all-done.2) | copy-start | bytes 18436
  13.2 10.9 %all-to-all-start.1 = ((bf16[4,2,384]{2,1,0:T(2,128)(2,1)}), bf16[4,2,384]{2,1,0:T(2,128)(2,1)S(1)}, u32[]{:S(2)}, u32[]{:S(2)}) async-start(bf16[4,2,384]{2,1,0:T(2,128)(2,1)} %reshape.649), calls=%async_computation.1 | async-start | bytes 12288 | tf_op jit(solution)/shard_map/all_to_all | solution.py:69
  24.0 5.8 %copy-start.4 = (bf16[256,768]{1,0:T(8,128)(2,1)S(1)}, bf16[256,768]{1,0:T(8,128)(2,1)}, u32[]{:S(2)}) copy-start(bf16[256,768]{1,0:T(8,128)(2,1)} %param.20) | copy-start | bytes 1179652
  24.0 13.0 %copy-start.11 = (s32[32,3]{0,1:T(4,128)S(1)}, s32[32,3]{0,1:T(4,128)}, u32[]{:S(2)}) copy-start(s32[32,3]{0,1:T(4,128)} %param.25) | copy-start | bytes 1156
  24.0 14.6 %copy-start = (s32[32]{0:T(128)S(1)}, s32[32]{0:T(128)}, u32[]{:S(2)}) copy-start(s32[32]{0:T(128)} %param.24) | copy-start | bytes 388
  24.6 72.4 %all-to-all-start = ((bf16[2,8,2,64,768]{4,3,2,0,1:T(8,128)(2,1)}), bf16[2,8,2,64,768]{4,3,2,0,1:T(8,128)(2,1)S(1)}, u32[]{:S(2)}, u32[]{:S(2)}) async-start(bf16[2,8,2,64,768]{4,3,2,0,1:T(8,128)(2,1)} %copy.154), calls=%async_computation | async-start | bytes 6291456 | tf_op jit(solution)/shard_map/all_to_all | solution.py:91
  31.6 62.7 %collective-permute-start = (bf16[2,64,768]{2,1,0:T(8,128)(2,1)}, bf16[2,64,768]{2,1,0:T(8,128)(2,1)}, u32[]{:S(2)}, u32[]{:S(2)}) collective-permute-start(bf16[2,64,768]{2,1,0:T(8,128)(2,1)} %get-tuple-element.79), channel_id=1, source_target_pairs={{0,4},{4,8},{8,12},{12,16},{16,20},{20,24},{24,28},{1,5},{5,9},{9,... | collective-permute-start | bytes 589832 | tf_op jit(solution)/shard_map/ppermute | solution.py:16
  35.1 59.1 %collective-permute-start.1 = (bf16[2,64,768]{2,1,0:T(8,128)(2,1)}, bf16[2,64,768]{2,1,0:T(8,128)(2,1)}, u32[]{:S(2)}, u32[]{:S(2)}) collective-permute-start(bf16[2,64,768]{2,1,0:T(8,128)(2,1)} %get-tuple-element.80), channel_id=1, source_target_pairs={{4,0},{8,4},{12,8},{16,12},{20,16},{24,20},{28,24},{5,1},{9,5},{13... | collective-permute-start | bytes 589832 | tf_op jit(solution)/shard_map/ppermute | solution.py:19
  116.1 4.2 %copy-start.8 = (bf16[2,32,6,128]{3,1,2,0:T(8,128)(2,1)S(1)}, bf16[2,32,6,128]{3,1,2,0:T(8,128)(2,1)}, u32[]{:S(2)}) copy-start(bf16[2,32,6,128]{3,1,2,0:T(8,128)(2,1)} %copy.161) | copy-start | bytes 294916
  116.1 4.2 %copy-start.7 = (bf16[4,64,6,128]{3,2,1,0:T(8,128)(2,1)S(1)}, bf16[4,64,6,128]{3,2,1,0:T(8,128)(2,1)}, u32[]{:S(2)}) copy-start(bf16[4,64,6,128]{3,2,1,0:T(8,128)(2,1)} %broadcast_select_fusion) | copy-start | bytes 1179652
  125.3 5.4 %copy-start.18 = (f32[4,6,64]{2,1,0:T(8,128)}, f32[4,6,64]{2,1,0:T(8,128)S(1)}, u32[]{:S(2)}) copy-start(f32[4,6,64]{2,1,0:T(8,128)S(1)} %get-tuple-element.88) | copy-start | bytes 18436
  145.7 4.2 %copy-start.3 = (f32[1,4,416,6,128]{4,2,3,1,0:T(8,128)S(1)}, f32[1,4,416,6,128]{4,2,3,1,0:T(8,128)}, u32[]{:S(2)}) copy-start(f32[1,4,416,6,128]{4,2,3,1,0:T(8,128)} %convolution_bitcast_fusion.2) | copy-start | bytes 15335428
  180.8 9.2 %all-to-all-start.5 = ((bf16[4,2,384]{2,1,0:T(2,128)(2,1)}), bf16[4,2,384]{2,1,0:T(2,128)(2,1)}, u32[]{:S(2)}, u32[]{:S(2)}) async-start(bf16[4,2,384]{2,1,0:T(2,128)(2,1)} %reshape.653), calls=%async_computation.5 | async-start | bytes 12288 | tf_op jit(solution)/shard_map/all_to_all | solution.py:180
  190.0 55.6 %all-to-all-start.4 = ((bf16[4,2,384]{2,1,0:T(2,128)(2,1)}), bf16[4,2,384]{2,1,0:T(2,128)(2,1)S(1)}, u32[]{:S(2)}, u32[]{:S(2)}) async-start(bf16[4,2,384]{2,1,0:T(2,128)(2,1)} %reshape.651), calls=%async_computation.4 | async-start | bytes 12288 | tf_op jit(solution)/shard_map/all_to_all | solution.py:179
  245.6 9.3 %copy-start.16 = (pred[4,64]{1,0:T(4,128)(4,1)S(1)}, pred[4,64]{1,0:T(4,128)(4,1)}, u32[]{:S(2)}) copy-start(pred[4,64]{1,0:T(4,128)(4,1)} %copy-done.15) | copy-start | bytes 772
  245.6 9.3 %copy-start.19 = (f32[4,6,64]{2,1,0:T(8,128)S(1)}, f32[4,6,64]{2,1,0:T(8,128)}, u32[]{:S(2)}) copy-start(f32[4,6,64]{2,1,0:T(8,128)} %copy-done.18) | copy-start | bytes 18436
  245.6 13.8 %slice-start = ((s8[9437184]{0:T(1024)(128)(4,1)}), s8[1048576]{0:T(1024)(128)(4,1)S(1)}, s32[]{:S(2)}) async-start(s8[9437184]{0:T(1024)(128)(4,1)} %bitcast.152), calls=%async_computation.6 | async-start | bytes 2097152
  245.6 53.8 %all-to-all-start.3 = ((bf16[2,8,2,64,768]{4,3,2,0,1:T(8,128)(2,1)}), bf16[2,8,2,64,768]{4,3,2,0,1:T(8,128)(2,1)}, u32[]{:S(2)}, u32[]{:S(2)}) async-start(bf16[2,8,2,64,768]{4,3,2,0,1:T(8,128)(2,1)} %copy.180), calls=%async_computation.3 | async-start | bytes 6291456 | tf_op jit(solution)/shard_map/all_to_all | solution.py:153
  254.9 4.6 %slice-start.1 = ((s8[9437184]{0:T(1024)(128)(4,1)}), s8[4194304]{0:T(1024)(128)(4,1)S(1)}, s32[]{:S(2)}) async-start(s8[9437184]{0:T(1024)(128)(4,1)} %bitcast.152), calls=%async_computation.7 | async-start | bytes 8388608
  254.9 5.2 %slice-start.2 = ((s8[9437184]{0:T(1024)(128)(4,1)}), s8[4194304]{0:T(1024)(128)(4,1)S(1)}, s32[]{:S(2)}) async-start(s8[9437184]{0:T(1024)(128)(4,1)} %bitcast.152), calls=%async_computation.8 | async-start | bytes 8388608
  261.8 33.7 %collective-permute-start.2 = (bf16[2,64,768]{2,1,0:T(8,128)(2,1)S(1)}, bf16[2,64,768]{2,1,0:T(8,128)(2,1)}, u32[]{:S(2)}, u32[]{:S(2)}) collective-permute-start(bf16[2,64,768]{2,1,0:T(8,128)(2,1)S(1)} %fusion.51), channel_id=1, source_target_pairs={{4,0},{8,4},{12,8},{16,12},{20,16},{24,20},{28,24},{5,1},{9,5},{13... | collective-permute-start | bytes 589832 | tf_op jit(solution)/shard_map/ppermute | solution.py:27
  264.1 32.4 %collective-permute-start.3 = (bf16[2,64,768]{2,1,0:T(8,128)(2,1)S(1)}, bf16[2,64,768]{2,1,0:T(8,128)(2,1)}, u32[]{:S(2)}, u32[]{:S(2)}) collective-permute-start(bf16[2,64,768]{2,1,0:T(8,128)(2,1)S(1)} %fusion.52), channel_id=1, source_target_pairs={{0,4},{4,8},{8,12},{12,16},{16,20},{20,24},{24,28},{1,5},{5,9},{9,... | collective-permute-start | bytes 589832 | tf_op jit(solution)/shard_map/ppermute | solution.py:27
  301.6 2.9 copy-start.13
  (9 other events, 17.7 us)
where the time goes:
time: 313 us; the launch traced here: 311 us
  local copies, waits for them, and re-layouts  115 us (37%)
  blocking collectives  45.6 us (15%)
  starting transfers between devices  43.7 us (14%)
  matrix products  41.5 us (13%)
  other arithmetic  34.1 us (11%)
  waiting for transfers between devices  28.7 us (9%)
    ppermute x2, waiting for transfers between devices, passed_along(): return lax.ppermute(x, axis, pairs)  26.2 us
    unnamed x1, blocking collectives  23.6 us
    unnamed x62, local copies, waits for them, and re-layouts  18 us
    dot_general x1, matrix products, block_terms(): jnp.einsum('ghqk,gqhd->gkhd', dscore, query, preferred_element_type=jnp.f...  14.9 us
    reshape x2, local copies, waits for them, and re-layouts, per_device(): near_kv = near_kv.reshape(2, group_size, near_count, head_count, DH)  14.9 us
    slice x1, local copies, waits for them, and re-layouts, per_device(): both_grad[:, :, :near_count].reshape(2, group_size, 3 + RAND, BLK, features)  13.6 us
    dot_general x1, matrix products, block_terms(): jnp.einsum('ghqk,gkhd->gqhd', dscore, all_keys, preferred_element_type=jn...  12.9 us
    reshape x1, local copies, waits for them, and re-layouts, per_device(): both_grad[:, :, :near_count].reshape(2, group_size, 3 + RAND, BLK, features)  12.5 us
  transfers between devices with their start and end apart: 10, of which 2 were waited for; matrix products, arithmetic and copies ran while one was open for 37% of the time, Pallas kernels for 0%

commit v1 on v0

--- a/solution.py
+++ b/solution.py
@@ -1,6 +1,10 @@
+import functools
+
 import jax
 import jax.numpy as jnp
 from jax import lax
+from jax.experimental import pallas as pl
+from jax.experimental.pallas import tpu as pltpu
 from jax.sharding import PartitionSpec as P
 
 DH = 128
@@ -189,6 +193,349 @@
     )
 
 
+NEG = -1e30
+EXTRA = 16
+MESH = pl.DeviceIdType.MESH
+F32 = jnp.float32
+BF16 = jnp.bfloat16
+
+
+def fused_kernel(
+    heads, n_head, blocks,
+    valid_ref, pattern_ref, q_ref, k_ref, v_ref, g_ref, sc_ref,
+    att_ref, gq_ref, gk_ref, gv_ref, sg_ref,
+    kv, grads, rsib, rdiag, rdir, bias, sbuf, dbuf, pbuf, dsbuf, kt, vt, glive,
+    sc_recv, sc_stage, sc_send,
+    ag_send, ag_recv, rs_send, rs_recv, sc_ssem, sc_rsem, sg_ssem, sg_rsem,
+):
+    rows = blocks * BLK
+    slot = rows + EXTRA
+    total = 8 * slot
+    p = lax.axis_index("seq")
+    hd = lax.axis_index("head")
+    nc = p + 1 - 2 * lax.rem(p, 2)
+    nx = p + 2 - 4 * lax.rem(lax.div(p, 2), 2)
+    ny = p + 4 - 8 * lax.rem(lax.div(p, 4), 2)
+    nd = nx + ny - p
+    flip = nc - p
+
+    barrier = pltpu.get_barrier_semaphore()
+    for target in (nc, nx, ny):
+        pl.semaphore_signal(barrier, inc=1, device_id={"seq": target}, device_id_type=MESH)
+    for d in range(1, n_head):
+        pl.semaphore_signal(
+            barrier, inc=1, device_id={"head": lax.rem(hd + d, n_head)}, device_id_type=MESH
+        )
+    pl.semaphore_wait(barrier, 3 + n_head - 1)
+
+    def at_slot(ref, h, q):
+        return ref.at[h, :, pl.ds(pl.multiple_of(q * slot, 16), slot), :]
+
+    def at_half(ref, h, half, q):
+        return ref.at[h, half, pl.ds(pl.multiple_of(q * slot, 16), slot), :]
+
+    def copy(src, dst, ssem, rsem, dev):
+        return pltpu.make_async_remote_copy(
+            src_ref=src, dst_ref=dst, send_sem=ssem, recv_sem=rsem,
+            device_id={"seq": dev}, device_id_type=MESH,
+        )
+
+    def ag(h, k, sending):
+        sent, dev, arrives = (
+            (p, nx, nx), (p, ny, ny), (p, nc, nc), (nx, ny, nd), (ny, nx, nd),
+            (nx, nc, nx + flip), (ny, nc, ny + flip), (nd, nc, nd + flip),
+        )[k]
+        s = sent if sending else arrives
+        ref = at_half(kv, h, k - 3, s) if k in (3, 4) else at_slot(kv, h, s)
+        return copy(ref, ref, ag_send.at[h, k], ag_recv.at[h, k], dev)
+
+    def rs(h, k):
+        if k < 4:
+            q = (p, nx, ny, nd)[k] + flip
+            src, dst, dev = at_slot(grads, h, q), rsib.at[h, k], nc
+        elif k < 6:
+            src, dst = at_half(grads, h, k - 4, nd), rdiag.at[h, k - 4]
+            dev = (nx, ny)[k - 4]
+        else:
+            dev = (nx, ny)[k - 6]
+            src, dst = at_slot(grads, h, dev), rdir.at[h, k - 6]
+        return copy(src, dst, rs_send.at[h, k], rs_recv.at[h, k], dev)
+
+    def scene(d, src, dst, ssem, rsem):
+        target = lax.rem(hd + d, n_head)
+        return pltpu.make_async_remote_copy(
+            src_ref=src.at[target], dst_ref=dst.at[hd], send_sem=ssem.at[d], recv_sem=rsem.at[d],
+            device_id={"head": target}, device_id_type=MESH,
+        )
+
+    for d in range(1, n_head):
+        scene(d, sc_ref, sc_recv, sc_ssem, sc_rsem).start()
+    sc_recv[hd] = sc_ref[hd]
+    own = pl.multiple_of(p * slot, 16)
+    for h in range(heads):
+        kv[h, 0, pl.ds(own, rows), :] = k_ref[:, h * DH:(h + 1) * DH]
+        kv[h, 1, pl.ds(own, rows), :] = v_ref[:, h * DH:(h + 1) * DH]
+    sc_stage[...] = jnp.zeros_like(sc_stage)
+    for d in range(1, n_head):
+        scene(d, sc_ref, sc_recv, sc_ssem, sc_rsem).wait()
+    for h in range(heads):
+        for half in range(2):
+            for t in range(n_head):
+                row = half * 8 + h
+                sc_stage[h, half, t:t + 1, :] = sc_recv[t, row:row + 1, :]
+            kv[h, half, pl.ds(pl.multiple_of(own + rows, 16), EXTRA), :] = sc_stage[
+                h, half
+            ].astype(BF16)
+    for h in range(min(2, heads)):
+        for k in range(3):
+            ag(h, k, True).start()
+
+    lane = lax.broadcasted_iota(jnp.int32, (1, rows), 1)
+    lane_block = lax.div(lane, BLK)
+    row_in = lax.broadcasted_iota(jnp.int32, (BLK, rows), 0)
+    named = []
+    for r in range(RAND):
+        row = jnp.zeros((1, rows), jnp.int32)
+        for b in range(blocks):
+            row = jnp.where(lane_block == b, pattern_ref[p * blocks + b, r], row)
+        named.append(row)
+    query_block = lane_block + p * blocks
+
+    def fill(c, carry):
+        gap = query_block - c
+        n = jnp.where((gap <= 1) & (gap >= -1), 1, 0)
+        for row in named:
+            n = n + jnp.where(row == c, 1, 0)
+        level = jnp.full((1, rows), NEG, F32)
+        for times, log in ((1, 0.0), (2, 0.6931471805599453), (3, 1.0986122886681098),
+                           (4, 1.3862943611198906)):
+            level = jnp.where(n == times, log, level)
+        at = pl.multiple_of(lax.div(c, blocks) * slot + lax.rem(c, blocks) * BLK, 16)
+        bias[pl.ds(at, BLK), :] = jnp.where(
+            row_in < valid_ref[c], jnp.broadcast_to(level, (BLK, rows)), NEG
+        )
+        return carry
+
+    lax.fori_loop(0, 8 * blocks, fill, 0)
+    extra_row = lax.broadcasted_iota(jnp.int32, (EXTRA, rows), 0)
+    for s in range(8):
+        bias[s * slot + rows:(s + 1) * slot, :] = jnp.where(extra_row < n_head, 0.0, NEG)
+
+    count = jnp.zeros((1, rows), jnp.int32)
+    for b in range(blocks):
+        count = jnp.where(lane_block == b, valid_ref[p * blocks + b], count)
+    live_lane = lane - lane_block * BLK < count
+    in_block = lax.broadcasted_iota(jnp.int32, (BLK, DH), 0)
+    for b in range(blocks):
+        keep = in_block < valid_ref[p * blocks + b]
+        for h in range(heads):
+            part = g_ref[b * BLK:(b + 1) * BLK, h * DH:(h + 1) * DH].astype(F32)
+            glive[b * BLK:(b + 1) * BLK, h * DH:(h + 1) * DH] = jnp.where(
+                keep, part, 0.0
+            ).astype(BF16)
+
+    scale = DH ** (-0.5)
+    piece = 128
+    pieces = total // piece
+
+    def attend(h):
+        cols = pl.ds(pl.multiple_of(h * DH, DH), DH)
+        q = q_ref[:, cols]
+        g = glive[:, cols]
+
+        def first(j, top):
+            at = pl.ds(pl.multiple_of(j * piece, piece), piece)
+            key = kv[h, 0, at, :]
+            s = lax.dot_general(key, q, (((1,), (1,)), ((), ())), preferred_element_type=F32)
+            s = s * scale + bias[at, :]
+            sbuf[at, :] = s
+            kt[:, at] = key.T
+            return jnp.maximum(top, jnp.max(s.reshape(piece // 8, 8, rows), axis=0))
+
+        top = lax.fori_loop(0, pieces, first, jnp.full((8, rows), NEG, F32), unroll=True)
+        top = jnp.max(top, axis=0, keepdims=True)
+
+        def second(j, sums):
+            at = pl.ds(pl.multiple_of(j * piece, piece), piece)
+            value = kv[h, 1, at, :]
+            e = jnp.exp(sbuf[at, :] - top)
+            dp = lax.dot_general(value, g, (((1,), (1,)), ((), ())), preferred_element_type=F32)
+            sbuf[at, :] = e
+            dbuf[at, :] = dp
+            vt[:, at] = value.T
+            z, delta = sums
+            z = z + jnp.sum(e.reshape(piece // 8, 8, rows), axis=0)
+            delta = delta + jnp.sum((e * dp).reshape(piece // 8, 8, rows), axis=0)
+            return z, delta
+
+        zero = jnp.zeros((8, rows), F32)
+        z, delta = lax.fori_loop(0, pieces, second, (zero, zero), unroll=True)
+        inv = 1.0 / jnp.sum(z, axis=0, keepdims=True)
+        delta = jnp.sum(delta, axis=0, keepdims=True) * inv
+
+        def third(j, carry):
+            at = pl.ds(pl.multiple_of(j * piece, piece), piece)
+            prob = sbuf[at, :] * inv
+            prob_b = prob.astype(BF16)
+            ds = (prob * (dbuf[at, :] - delta) * scale).astype(BF16)
+            pbuf[at, :] = prob_b
+            dsbuf[at, :] = ds
+            grads[h, 0, at, :] = jnp.dot(ds, q, preferred_element_type=F32).astype(BF16)
+            grads[h, 1, at, :] = jnp.dot(prob_b, g, preferred_element_type=F32).astype(BF16)
+            return carry
+
+        lax.fori_loop(0, pieces, third, 0, unroll=True)
+        out = jnp.dot(vt[...], pbuf[...], preferred_element_type=F32)
+        att_ref[:, cols] = jnp.where(live_lane, out, 0.0).T.astype(BF16)
+        gq = jnp.dot(kt[...], dsbuf[...], preferred_element_type=F32)
+        gq_ref[:, cols] = gq.T.astype(BF16)
+
+    def part(h, half, q):
+        return grads[h, half, pl.ds(pl.multiple_of(q * slot, 16), slot), :].astype(F32)
+
+    def keep_part(h, half, q, x):
+        grads[h, half, pl.ds(pl.multiple_of(q * slot, 16), slot), :] = x.astype(BF16)
+
+    def step(t, carry):
+        @pl.when(t < heads)
+        def _():
+            ag(t, 0, False).wait_recv()
+            ag(t, 1, False).wait_recv()
+            for k in (3, 4, 5, 6):
+                ag(t, k, True).start()
+
+        @pl.when(t + 2 < heads)
+        def _():
+            for k in range(3):
+                ag(t + 2, k, True).start()
+
+        @pl.when((t >= 1) & (t < heads + 1))
+        def _():
+            ag(t - 1, 3, False).wait_recv()
+            ag(t - 1, 4, False).wait_recv()
+            ag(t - 1, 7, True).start()
+
+        @pl.when((t >= 3) & (t < heads + 3))
+        def _():
+            h = t - 3
+            for k in range(4):
+                rs(h, k).wait_recv()
+            for half in range(2):
+                keep_part(h, half, nd, part(h, half, nd) + rsib[h, 3, half].astype(F32))
+            rs(h, 4).start()
+            rs(h, 5).start()
+
+        @pl.when((t >= 4) & (t < heads + 4))
+        def _():
+            h = t - 4
+            rs(h, 4).wait_recv()
+            rs(h, 5).wait_recv()
+            for k, q, half_in in ((1, nx, 1), (2, ny, 0)):
+                for half in range(2):
+                    x = part(h, half, q) + rsib[h, k, half].astype(F32)
+                    if half == half_in:
+                        x = x + rdiag[h, half].astype(F32)
+                    keep_part(h, half, q, x)
+                rs(h, 5 + k).start()
+
+        @pl.when((t >= 2) & (t < heads + 2))
+        def _():
+            h = t - 2
+            for k in (2, 5, 6, 7):
+                ag(h, k, False).wait_recv()
+            attend(h)
+            for k in range(4):
+                rs(h, k).start()
+
+        @pl.when(t >= 5)
+        def _():
+            h = t - 5
+            rs(h, 6).wait_recv()
+            rs(h, 7).wait_recv()
+            cols = pl.ds(pl.multiple_of(h * DH, DH), DH)
+            for half, ref in ((0, gk_ref), (1, gv_ref)):
+                x = part(h, half, p) + rsib[h, 0, half].astype(F32)
+                x = x + rdir[h, 0, half].astype(F32) + rdir[h, 1, half].astype(F32)
+                ref[:, cols] = x[:rows].astype(BF16)
+                sc_stage[h, half] = x[rows:]
+
+        return carry
+
+    lax.fori_loop(0, heads + 5, step, 0)
+
+    sc_send[...] = jnp.zeros_like(sc_send)
+    for h in range(heads):
+        for half in range(2):
+            for t in range(n_head):
+                row = half * 8 + h
+                sc_send[t, row:row + 1, :] = sc_stage[h, half, t:t + 1, :]
+    for d in range(1, n_head):
+        scene(d, sc_send, sg_ref, sg_ssem, sg_rsem).start()
+    sg_ref[hd] = sc_send[hd]
+    for d in range(1, n_head):
+        scene(d, sc_send, sg_ref, sg_ssem, sg_rsem).wait()
+
+    def drain(h, carry):
+        for k in range(8):
+            ag(h, k, True).wait_send()
+            rs(h, k).wait_send()
+        return carry
+
+    lax.fori_loop(0, heads, drain, 0)
+
+
+def fused_device(queries, keys, values, grad_out, scene_keys, scene_values, valid, pattern):
+    n_head = lax.axis_size("head")
+    rows, features = queries.shape
+    heads = features // DH
+    blocks = rows // BLK
+    slot = rows + EXTRA
+    total = 8 * slot
+
+    def tile(x):
+        x = x.astype(F32).reshape(n_head, heads, DH)
+        return jnp.pad(x, ((0, 0), (0, 8 - heads), (0, 0)))
+
+    scene = jnp.concatenate([tile(scene_keys), tile(scene_values)], axis=1)
+    vmem = pl.BlockSpec(memory_space=pltpu.VMEM)
+    smem = pl.BlockSpec(memory_space=pltpu.SMEM)
+    wide = jax.ShapeDtypeStruct((rows, features), BF16)
+    dma = pltpu.SemaphoreType.DMA
+    out = pl.pallas_call(
+        functools.partial(fused_kernel, heads, n_head, blocks),
+        out_shape=[wide] * 4 + [jax.ShapeDtypeStruct((n_head, 16, DH), F32)],
+        in_specs=[smem, smem] + [vmem] * 5,
+        out_specs=[vmem] * 5,
+        scratch_shapes=[
+            pltpu.VMEM((heads, 2, total, DH), BF16),
+            pltpu.VMEM((heads, 2, total, DH), BF16),
+            pltpu.VMEM((heads, 4, 2, slot, DH), BF16),
+            pltpu.VMEM((heads, 2, slot, DH), BF16),
+            pltpu.VMEM((heads, 2, 2, slot, DH), BF16),
+            pltpu.VMEM((total, rows), F32),
+            pltpu.VMEM((total, rows), F32),
+            pltpu.VMEM((total, rows), F32),
+            pltpu.VMEM((total, rows), BF16),
+            pltpu.VMEM((total, rows), BF16),
+            pltpu.VMEM((DH, total), BF16),
+            pltpu.VMEM((DH, total), BF16),
+            pltpu.VMEM((rows, features), BF16),
+            pltpu.VMEM((n_head, 16, DH), F32),
+            pltpu.VMEM((heads, 2, EXTRA, DH), F32),
+            pltpu.VMEM((n_head, 16, DH), F32),
+            dma((heads, 8)), dma((heads, 8)), dma((heads, 8)), dma((heads, 8)),
+            dma((n_head,)), dma((n_head,)), dma((n_head,)), dma((n_head,)),
+        ],
+        compiler_params=pltpu.CompilerParams(
+            collective_id=0, has_side_effects=True, vmem_limit_bytes=52 * 1024 * 1024
+        ),
+    )(valid, pattern, queries, keys, values, grad_out, scene)
+    att, gq, gk, gv, sg = out
+    gsk = sg[:, :heads].reshape(1, n_head * features).astype(BF16)
+    gsv = sg[:, 8:8 + heads].reshape(1, n_head * features).astype(BF16)
+    return att, gq, gk, gv, gsk, gsv
+
+
 def solution(mesh):
     placed = (
         P("seq", "head"),
@@ -200,8 +547,9 @@
         P(),
         P(),
     )
+    body = fused_device if mesh.shape["seq"] == 8 else per_device
     return jax.shard_map(
-        per_device,
+        body,
         mesh=mesh,
         in_specs=placed,
         out_specs=(

time: 313 us -> 79.2 us (0.25)
  the two profiles are of different devices: /device:TPU:1 before, /device:TPU:0 now
where the time goes in v1:
time: 79.2 us; the launch traced here: 78.9 us
  Pallas kernels  71.9 us (91%)
  local copies, waits for them, and re-layouts  5.56 us (7%)
  other arithmetic  0.81 us (1%)
    pallas_call x1, Pallas kernels, fused_device(): pl.pallas_call(functools.partial(fused_kernel, heads, n_head, blocks), ou...  71.9 us
    unnamed x11, local copies, waits for them, and re-layouts  4.3 us

profile of v1, /device:TPU:0, one launch (start us, length us, event | category | flops | bytes accessed | tf_op | source)
XLA Modules:
  0.0 78.9 jit_solution(13490939543053713805)
XLA Ops:
  0.6 0.0 copy-start.1
  0.6 0.8 reduce
  1.4 0.0 copy-done.1
  1.5 0.0 copy-start.2
  1.5 0.7 copy-done.2
  2.2 0.0 copy-start
  2.2 0.1 copy.15.pattern_ref
  2.3 0.6 copy-done
  2.8 71.9 %shard_map.127 = (bf16[256,768]{1,0:T(8,128)(2,1)S(1)}, bf16[256,768]{1,0:T(8,128)(2,1)S(1)}, bf16[256,768]{1,0:T(8,128)(2,1)S(1)}, bf16[256,768]{1,0:T(8,128)(2,1)S(1)}, f32[4,16,128]{2,1,0:T(8,128)S(1)}) custom-call(s32[32]{0:T(128)S(1)} %copy-done, s32[32,3]{1,0:T(8,128)S(1)} %copy.15.pattern_ref, bf16[256,768]{1,0:T(8,128)(2,1)} %q_ref.1, ...), custom_call_target="tpu_custom_call" | custom-call | tf_op jit(solution)/shard_map/pallas_call | solution.py:504
  74.7 0.6 convert_element_type.29
  75.3 0.6 convert_element_type.30
  75.9 0.7 copy.20
  76.7 0.7 copy.21
  77.4 0.7 copy.22
  78.2 0.7 copy.23
  (6 shorter events, 0.1 us)
Async XLA Ops:
  0.6 0.8 copy-start.1
  1.5 0.7 copy-start.2
  2.2 0.7 copy-start

commit v2 on v1

--- a/solution.py
+++ b/solution.py
@@ -194,7 +194,7 @@
 
 
 NEG = -1e30
-EXTRA = 16
+SCENE_ROWS = 128
 MESH = pl.DeviceIdType.MESH
 F32 = jnp.float32
 BF16 = jnp.bfloat16
@@ -202,15 +202,18 @@
 
 def fused_kernel(
     heads, n_head, blocks,
-    valid_ref, pattern_ref, q_ref, k_ref, v_ref, g_ref, sc_ref,
+    valid_ref, pattern_ref, q_ref, k_ref, v_ref, g_ref, sk_ref, sv_ref,
     att_ref, gq_ref, gk_ref, gv_ref, sg_ref,
     kv, grads, rsib, rdiag, rdir, bias, sbuf, dbuf, pbuf, dsbuf, kt, vt, glive,
-    sc_recv, sc_stage, sc_send,
+    sc_src, sc_recv, sc_send, scx, sc_all, scg, srsib, srdiag, srdir,
     ag_send, ag_recv, rs_send, rs_recv, sc_ssem, sc_rsem, sg_ssem, sg_rsem,
+    sx_send, sx_recv, sr_send, sr_recv,
 ):
     rows = blocks * BLK
-    slot = rows + EXTRA
-    total = 8 * slot
+    slot = rows
+    base = 8 * slot
+    total = base + SCENE_ROWS
+    tokens = 8 * n_head
     p = lax.axis_index("seq")
     hd = lax.axis_index("head")
     nc = p + 1 - 2 * lax.rem(p, 2)
@@ -218,6 +221,11 @@
     ny = p + 4 - 8 * lax.rem(lax.div(p, 4), 2)
     nd = nx + ny - p
     flip = nc - p
+    own = pl.multiple_of(p * slot, 16)
+
+    def pack(h):
+        kv[h, 0, pl.ds(own, rows), :] = k_ref[:, h * DH:(h + 1) * DH]
+        kv[h, 1, pl.ds(own, rows), :] = v_ref[:, h * DH:(h + 1) * DH]
 
     barrier = pltpu.get_barrier_semaphore()
     for target in (nc, nx, ny):
@@ -226,6 +234,14 @@
         pl.semaphore_signal(
             barrier, inc=1, device_id={"head": lax.rem(hd + d, n_head)}, device_id_type=MESH
         )
+    for h in range(min(2, heads)):
+        pack(h)
+    sc_src[...] = jnp.zeros_like(sc_src)
+    for t in range(n_head):
+        for h in range(heads):
+            at = (t * heads + h) * DH
+            sc_src[t, h:h + 1, :] = sk_ref[:, at:at + DH].astype(F32)
+            sc_src[t, 8 + h:9 + h, :] = sv_ref[:, at:at + DH].astype(F32)
     pl.semaphore_wait(barrier, 3 + n_head - 1)
 
     def at_slot(ref, h, q):
@@ -268,27 +284,43 @@
             device_id={"head": target}, device_id_type=MESH,
         )
 
+    def scene_gather(k, sending):
+        sent, dev, arrives = (
+            (p, nx, nx), (p, ny, ny), (p, nc, nc), (nx, ny, nd),
+            (nx, nc, nx + flip), (ny, nc, ny + flip), (nd, nc, nd + flip),
+        )[k]
+        ref = scx.at[sent if sending else arrives]
+        return copy(ref, ref, sx_send.at[k], sx_recv.at[k], dev)
+
+    def scene_sum(k):
+        src, dst, dev = (
+            (nc, srsib.at[0], nc), (nx + flip, srsib.at[1], nc), (ny + flip, srsib.at[2], nc),
+            (nd + flip, srsib.at[3], nc), (nd, srdiag, nx), (nx, srdir.at[0], nx),
+            (ny, srdir.at[1], ny),
+        )[k]
+        return copy(scg.at[src], dst, sr_send.at[k], sr_recv.at[k], dev)
+
+    def scene_row(h, half):
+        return (half * heads + h) * n_head
+
     for d in range(1, n_head):
-        scene(d, sc_ref, sc_recv, sc_ssem, sc_rsem).start()
-    sc_recv[hd] = sc_ref[hd]
-    own = pl.multiple_of(p * slot, 16)
-    for h in range(heads):
-        kv[h, 0, pl.ds(own, rows), :] = k_ref[:, h * DH:(h + 1) * DH]
-        kv[h, 1, pl.ds(own, rows), :] = v_ref[:, h * DH:(h + 1) * DH]
-    sc_stage[...] = jnp.zeros_like(sc_stage)
+        scene(d, sc_src, sc_recv, sc_ssem, sc_rsem).start()
+    for h in range(min(2, heads)):
+        for k in range(3):
+            ag(h, k, True).start()
+    sc_recv[hd] = sc_src[hd]
+    for h in range(2, heads):
+        pack(h)
     for d in range(1, n_head):
-        scene(d, sc_ref, sc_recv, sc_ssem, sc_rsem).wait()
+        scene(d, sc_src, sc_recv, sc_ssem, sc_rsem).wait()
     for h in range(heads):
         for half in range(2):
             for t in range(n_head):
                 row = half * 8 + h
-                sc_stage[h, half, t:t + 1, :] = sc_recv[t, row:row + 1, :]
-            kv[h, half, pl.ds(pl.multiple_of(own + rows, 16), EXTRA), :] = sc_stage[
-                h, half
-            ].astype(BF16)
-    for h in range(min(2, heads)):
-        for k in range(3):
-            ag(h, k, True).start()
+                at = scene_row(h, half) + t
+                scx[p, at:at + 1, :] = sc_recv[t, row:row + 1, :]
+    for k in range(3):
+        scene_gather(k, True).start()
 
     lane = lax.broadcasted_iota(jnp.int32, (1, rows), 1)
     lane_block = lax.div(lane, BLK)
@@ -310,16 +342,22 @@
         for times, log in ((1, 0.0), (2, 0.6931471805599453), (3, 1.0986122886681098),
                            (4, 1.3862943611198906)):
             level = jnp.where(n == times, log, level)
-        at = pl.multiple_of(lax.div(c, blocks) * slot + lax.rem(c, blocks) * BLK, 16)
+        at = pl.multiple_of(c * BLK, BLK)
         bias[pl.ds(at, BLK), :] = jnp.where(
             row_in < valid_ref[c], jnp.broadcast_to(level, (BLK, rows)), NEG
         )
         return carry
 
     lax.fori_loop(0, 8 * blocks, fill, 0)
-    extra_row = lax.broadcasted_iota(jnp.int32, (EXTRA, rows), 0)
-    for s in range(8):
-        bias[s * slot + rows:(s + 1) * slot, :] = jnp.where(extra_row < n_head, 0.0, NEG)
+    scene_gather(0, False).wait_recv()
+    scene_gather(1, False).wait_recv()
+    for k in (3, 4, 5):
+        scene_gather(k, True).start()
+    extra_row = lax.broadcasted_iota(jnp.int32, (SCENE_ROWS, rows), 0)
+    bias[base:, :] = jnp.where(extra_row < tokens, 0.0, NEG)
+    for h in range(heads):
+        for half in range(2):
+            kv[h, half, base + tokens:, :] = jnp.zeros((SCENE_ROWS - tokens, DH), BF16)
 
     count = jnp.zeros((1, rows), jnp.int32)
     for b in range(blocks):
@@ -334,8 +372,19 @@
                 keep, part, 0.0
             ).astype(BF16)
 
+    scene_gather(3, False).wait_recv()
+    scene_gather(6, True).start()
+    for k in (2, 4, 5, 6):
+        scene_gather(k, False).wait_recv()
+    for h in range(heads):
+        for half in range(2):
+            for i in range(8):
+                at = scene_row(h, half)
+                sc_all[h, half, i * n_head:(i + 1) * n_head, :] = scx[i, at:at + n_head, :]
+            kv[h, half, base:base + tokens, :] = sc_all[h, half].astype(BF16)
+
     scale = DH ** (-0.5)
-    piece = 128
+    piece = SCENE_ROWS
     pieces = total // piece
 
     def attend(h):
@@ -373,18 +422,27 @@
         inv = 1.0 / jnp.sum(z, axis=0, keepdims=True)
         delta = jnp.sum(delta, axis=0, keepdims=True) * inv
 
-        def third(j, carry):
+        def terms(j):
             at = pl.ds(pl.multiple_of(j * piece, piece), piece)
             prob = sbuf[at, :] * inv
             prob_b = prob.astype(BF16)
             ds = (prob * (dbuf[at, :] - delta) * scale).astype(BF16)
             pbuf[at, :] = prob_b
             dsbuf[at, :] = ds
-            grads[h, 0, at, :] = jnp.dot(ds, q, preferred_element_type=F32).astype(BF16)
-            grads[h, 1, at, :] = jnp.dot(prob_b, g, preferred_element_type=F32).astype(BF16)
+            grad_k = jnp.dot(ds, q, preferred_element_type=F32)
+            grad_v = jnp.dot(prob_b, g, preferred_element_type=F32)
+            return at, grad_k, grad_v
+
+        def third(j, carry):
+            at, grad_k, grad_v = terms(j)
+            grads[h, 0, at, :] = grad_k.astype(BF16)
+            grads[h, 1, at, :] = grad_v.astype(BF16)
             return carry
 
-        lax.fori_loop(0, pieces, third, 0, unroll=True)
+        lax.fori_loop(0, pieces - 1, third, 0, unroll=True)
+        _, grad_k, grad_v = terms(pieces - 1)
+        sc_all[h, 0] = grad_k[:tokens]
+        sc_all[h, 1] = grad_v[:tokens]
         out = jnp.dot(vt[...], pbuf[...], preferred_element_type=F32)
         att_ref[:, cols] = jnp.where(live_lane, out, 0.0).T.astype(BF16)
         gq = jnp.dot(kt[...], dsbuf[...], preferred_element_type=F32)
@@ -456,19 +514,49 @@
             for half, ref in ((0, gk_ref), (1, gv_ref)):
                 x = part(h, half, p) + rsib[h, 0, half].astype(F32)
                 x = x + rdir[h, 0, half].astype(F32) + rdir[h, 1, half].astype(F32)
-                ref[:, cols] = x[:rows].astype(BF16)
-                sc_stage[h, half] = x[rows:]
+                ref[:, cols] = x.astype(BF16)
+
+        @pl.when(t == heads + 1)
+        def _():
+            for h in range(heads):
+                for half in range(2):
+                    at = scene_row(h, half)
+                    for i in range(8):
+                        scg[i, at:at + n_head, :] = sc_all[
+                            h, half, i * n_head:(i + 1) * n_head, :
+                        ]
+            for k in range(4):
+                scene_sum(k).start()
+
+        @pl.when(t == heads + 2)
+        def _():
+            for k in range(4):
+                scene_sum(k).wait_recv()
+            scg[nd] = scg[nd] + srsib[3]
+            scene_sum(4).start()
+
+        @pl.when(t == heads + 3)
+        def _():
+            scene_sum(4).wait_recv()
+            scg[nx] = scg[nx] + srsib[1]
+            scg[ny] = scg[ny] + srsib[2] + srdiag[...]
+            scene_sum(5).start()
+            scene_sum(6).start()
 
         return carry
 
     lax.fori_loop(0, heads + 5, step, 0)
 
+    scene_sum(5).wait_recv()
+    scene_sum(6).wait_recv()
+    scg[p] = scg[p] + srsib[0] + srdir[0] + srdir[1]
     sc_send[...] = jnp.zeros_like(sc_send)
     for h in range(heads):
         for half in range(2):
             for t in range(n_head):
                 row = half * 8 + h
-                sc_send[t, row:row + 1, :] = sc_stage[h, half, t:t + 1, :]
+                at = scene_row(h, half) + t
+                sc_send[t, row:row + 1, :] = scg[p, at:at + 1, :]
     for d in range(1, n_head):
         scene(d, sc_send, sg_ref, sg_ssem, sg_rsem).start()
     sg_ref[hd] = sc_send[hd]
@@ -482,6 +570,21 @@
         return carry
 
     lax.fori_loop(0, heads, drain, 0)
+    for k in range(7):
+        scene_gather(k, True).wait_send()
+        scene_sum(k).wait_send()
+
+
+def finish_kernel(heads, n_head, a_ref, b_ref, c_ref, d_ref, sg_ref, ao, bo, co, do, sko, svo):
+    ao[...] = a_ref[...]
+    bo[...] = b_ref[...]
+    co[...] = c_ref[...]
+    do[...] = d_ref[...]
+    for t in range(n_head):
+        for h in range(heads):
+            at = (t * heads + h) * DH
+            sko[:, at:at + DH] = sg_ref[t, h:h + 1, :].astype(BF16)
+            svo[:, at:at + DH] = sg_ref[t, 8 + h:9 + h, :].astype(BF16)
 
 
 def fused_device(queries, keys, values, grad_out, scene_keys, scene_values, valid, pattern):
@@ -489,14 +592,11 @@
     rows, features = queries.shape
     heads = features // DH
     blocks = rows // BLK
-    slot = rows + EXTRA
-    total = 8 * slot
-
-    def tile(x):
-        x = x.astype(F32).reshape(n_head, heads, DH)
-        return jnp.pad(x, ((0, 0), (0, 8 - heads), (0, 0)))
-
-    scene = jnp.concatenate([tile(scene_keys), tile(scene_values)], axis=1)
+    slot = rows
+    base = 8 * slot
+    total = base + SCENE_ROWS
+    tokens = 8 * n_head
+    flat = 2 * heads * n_head
     vmem = pl.BlockSpec(memory_space=pltpu.VMEM)
     smem = pl.BlockSpec(memory_space=pltpu.SMEM)
     wide = jax.ShapeDtypeStruct((rows, features), BF16)
@@ -504,11 +604,11 @@
     out = pl.pallas_call(
         functools.partial(fused_kernel, heads, n_head, blocks),
         out_shape=[wide] * 4 + [jax.ShapeDtypeStruct((n_head, 16, DH), F32)],
-        in_specs=[smem, smem] + [vmem] * 5,
+        in_specs=[smem, smem] + [vmem] * 6,
         out_specs=[vmem] * 5,
         scratch_shapes=[
             pltpu.VMEM((heads, 2, total, DH), BF16),
-            pltpu.VMEM((heads, 2, total, DH), BF16),
+            pltpu.VMEM((heads, 2, base, DH), BF16),
             pltpu.VMEM((heads, 4, 2, slot, DH), BF16),
             pltpu.VMEM((heads, 2, slot, DH), BF16),
             pltpu.VMEM((heads, 2, 2, slot, DH), BF16),
@@ -521,19 +621,31 @@
             pltpu.VMEM((DH, total), BF16),
             pltpu.VMEM((rows, features), BF16),
             pltpu.VMEM((n_head, 16, DH), F32),
-            pltpu.VMEM((heads, 2, EXTRA, DH), F32),
             pltpu.VMEM((n_head, 16, DH), F32),
+            pltpu.VMEM((n_head, 16, DH), F32),
+            pltpu.VMEM((8, flat, DH), F32),
+            pltpu.VMEM((heads, 2, tokens, DH), F32),
+            pltpu.VMEM((8, flat, DH), F32),
+            pltpu.VMEM((4, flat, DH), F32),
+            pltpu.VMEM((flat, DH), F32),
+            pltpu.VMEM((2, flat, DH), F32),
             dma((heads, 8)), dma((heads, 8)), dma((heads, 8)), dma((heads, 8)),
             dma((n_head,)), dma((n_head,)), dma((n_head,)), dma((n_head,)),
+            dma((7,)), dma((7,)), dma((7,)), dma((7,)),
         ],
         compiler_params=pltpu.CompilerParams(
             collective_id=0, has_side_effects=True, vmem_limit_bytes=52 * 1024 * 1024
         ),
-    )(valid, pattern, queries, keys, values, grad_out, scene)
-    att, gq, gk, gv, sg = out
-    gsk = sg[:, :heads].reshape(1, n_head * features).astype(BF16)
-    gsv = sg[:, 8:8 + heads].reshape(1, n_head * features).astype(BF16)
-    return att, gq, gk, gv, gsk, gsv
+    )(valid, pattern, queries, keys, values, grad_out, scene_keys, scene_values)
+    row = jax.ShapeDtypeStruct((1, n_head * features), BF16)
+    return tuple(
+        pl.pallas_call(
+            functools.partial(finish_kernel, heads, n_head),
+            out_shape=[wide] * 4 + [row] * 2,
+            in_specs=[vmem] * 5,
+            out_specs=[vmem] * 6,
+        )(*out)
+    )
 
 
 def solution(mesh):

time: 79.2 us -> 80.6 us (1.018)
  Pallas kernels: 71.9 us -> 74.5 us
  other arithmetic: 0.81 us -> 0 us
    pallas_call x0 -> x1, Pallas kernels: none -> 2.52 us  [fused_device(): pl.pallas_call(functools.partial(finish_kernel, heads, n_head), out_shape...]
    convert_element_type x2 -> x0, local copies, waits for them, and re-layouts: 1.23 us -> none  [the longest x1 0.62 us: fused_device(): gsk = sg[:, :heads].reshape(1, n_head * features).astype(BF16)]
    unnamed x11 -> x17, local copies, waits for them, and re-layouts: 4.3 us -> 5.11 us
where the time goes in v2:
time: 80.6 us; the launch traced here: 80.3 us
  Pallas kernels  74.5 us (92%)
  local copies, waits for them, and re-layouts  5.11 us (6%)
    pallas_call x1, Pallas kernels, fused_device(): pl.pallas_call(functools.partial(fused_kernel, heads, n_head, blocks), ou...  72 us
    unnamed x17, local copies, waits for them, and re-layouts  5.11 us
    pallas_call x1, Pallas kernels, fused_device(): pl.pallas_call(functools.partial(finish_kernel, heads, n_head), out_shape...  2.52 us

profile of v2, /device:TPU:0, one launch (start us, length us, event | category | flops | bytes accessed | tf_op | source)
XLA Modules:
  0.0 80.3 jit_solution(5740185275099662495)
XLA Ops:
  0.6 0.0 copy-start.7
  0.6 0.0 copy-start.5
  0.7 0.8 copy.14.pattern_ref
  1.4 0.0 copy-done.7
  1.4 0.0 copy-done.5
  1.4 0.0 copy-start.6
  1.4 0.7 copy-done.6
  2.1 72.0 %shard_map.127 = (bf16[256,768]{1,0:T(8,128)(2,1)S(1)}, bf16[256,768]{1,0:T(8,128)(2,1)S(1)}, bf16[256,768]{1,0:T(8,128)(2,1)S(1)}, bf16[256,768]{1,0:T(8,128)(2,1)S(1)}, f32[4,16,128]{2,1,0:T(8,128)S(1)}) custom-call(s32[32]{0:T(128)S(1)} %copy-done.7, s32[32,3]{1,0:T(8,128)S(1)} %copy.14.pattern_ref, bf16[256,768]{1,0:T(8,128)(2,1)} %q_ref.1, ...), custom_call_target="tpu_custom_call" | custom-call | tf_op jit(solution)/shard_map/pallas_call | solution.py:604
  74.1 0.0 copy-start
  74.1 0.7 copy-done
  74.9 0.0 copy-start.1
  74.9 0.8 copy-done.1
  75.6 0.0 copy-start.2
  75.6 0.8 copy-done.2
  76.4 0.0 copy-start.3
  76.4 0.8 copy-done.3
  77.2 0.0 copy-start.4
  77.2 0.6 copy-done.4
  77.8 2.5 %shard_map.128 = (bf16[256,768]{1,0:T(8,128)(2,1)}, bf16[256,768]{1,0:T(8,128)(2,1)}, bf16[256,768]{1,0:T(8,128)(2,1)}, bf16[256,768]{1,0:T(8,128)(2,1)}, bf16[1...) custom-call(bf16[256,768]{1,0:T(8,128)(2,1)} %copy-done, bf16[256,768]{1,0:T(8,128)(2,1)} %copy-done.1, ...), custom_call_target="tpu_custom_call" | custom-call | tf_op jit(solution)/shard_map/pallas_call | solution.py:642
Async XLA Ops:
  0.6 0.8 copy-start.7
  0.6 0.8 copy-start.5
  1.4 0.7 copy-start.6
  74.1 0.7 copy-start
  74.9 0.8 copy-start.1
  75.6 0.8 copy-start.2
  76.4 0.8 copy-start.3
  77.2 0.6 copy-start.4

commit v3 on v2

--- a/solution.py
+++ b/solution.py
@@ -204,7 +204,7 @@
     heads, n_head, blocks,
     valid_ref, pattern_ref, q_ref, k_ref, v_ref, g_ref, sk_ref, sv_ref,
     att_ref, gq_ref, gk_ref, gv_ref, sg_ref,
-    kv, grads, rsib, rdiag, rdir, bias, sbuf, dbuf, pbuf, dsbuf, kt, vt, glive,
+    kv, grads, rsib, rdiag, rdir, bias, sbuf, dbuf, pbuf, dsbuf, kt, vt, glive, qt, gt,
     sc_src, sc_recv, sc_send, scx, sc_all, scg, srsib, srdiag, srdir,
     ag_send, ag_recv, rs_send, rs_recv, sc_ssem, sc_rsem, sg_ssem, sg_rsem,
     sx_send, sx_recv, sr_send, sr_recv,
@@ -339,8 +339,7 @@
         for row in named:
             n = n + jnp.where(row == c, 1, 0)
         level = jnp.full((1, rows), NEG, F32)
-        for times, log in ((1, 0.0), (2, 0.6931471805599453), (3, 1.0986122886681098),
-                           (4, 1.3862943611198906)):
+        for times, log in ((1, 0.0), (2, 1.0), (3, 1.584962500721156), (4, 2.0)):
             level = jnp.where(n == times, log, level)
         at = pl.multiple_of(c * BLK, BLK)
         bias[pl.ds(at, BLK), :] = jnp.where(
@@ -372,6 +371,9 @@
                 keep, part, 0.0
             ).astype(BF16)
 
+    for h in range(heads):
+        qt[h] = q_ref[:, h * DH:(h + 1) * DH].T
+        gt[h] = glive[:, h * DH:(h + 1) * DH].T
     scene_gather(3, False).wait_recv()
     scene_gather(6, True).start()
     for k in (2, 4, 5, 6):
@@ -384,65 +386,60 @@
             kv[h, half, base:base + tokens, :] = sc_all[h, half].astype(BF16)
 
     scale = DH ** (-0.5)
-    piece = SCENE_ROWS
-    pieces = total // piece
+    scale2 = scale * 1.4426950408889634
+    pieces = [(i * rows, rows) for i in range(8)] + [(base, SCENE_ROWS)]
+
+    def folded(x, op):
+        return op(x.reshape(x.shape[0] // 8, 8, rows), axis=0)
 
     def attend(h):
         cols = pl.ds(pl.multiple_of(h * DH, DH), DH)
-        q = q_ref[:, cols]
-        g = glive[:, cols]
-
-        def first(j, top):
-            at = pl.ds(pl.multiple_of(j * piece, piece), piece)
+        q_t = qt[h]
+        g_t = gt[h]
+        top = jnp.full((8, rows), NEG, F32)
+        for start, size in pieces:
+            at = slice(start, start + size)
             key = kv[h, 0, at, :]
-            s = lax.dot_general(key, q, (((1,), (1,)), ((), ())), preferred_element_type=F32)
-            s = s * scale + bias[at, :]
+            s = jnp.dot(key, q_t, preferred_element_type=F32) * scale2 + bias[at, :]
             sbuf[at, :] = s
             kt[:, at] = key.T
-            return jnp.maximum(top, jnp.max(s.reshape(piece // 8, 8, rows), axis=0))
-
-        top = lax.fori_loop(0, pieces, first, jnp.full((8, rows), NEG, F32), unroll=True)
+            top = jnp.maximum(top, folded(s, jnp.max))
         top = jnp.max(top, axis=0, keepdims=True)
-
-        def second(j, sums):
-            at = pl.ds(pl.multiple_of(j * piece, piece), piece)
+        z = jnp.zeros((8, rows), F32)
+        delta = jnp.zeros((8, rows), F32)
+        for start, size in pieces:
+            at = slice(start, start + size)
             value = kv[h, 1, at, :]
-            e = jnp.exp(sbuf[at, :] - top)
-            dp = lax.dot_general(value, g, (((1,), (1,)), ((), ())), preferred_element_type=F32)
+            e = jnp.exp2(sbuf[at, :] - top)
+            dp = jnp.dot(value, g_t, preferred_element_type=F32)
             sbuf[at, :] = e
             dbuf[at, :] = dp
             vt[:, at] = value.T
-            z, delta = sums
-            z = z + jnp.sum(e.reshape(piece // 8, 8, rows), axis=0)
-            delta = delta + jnp.sum((e * dp).reshape(piece // 8, 8, rows), axis=0)
-            return z, delta
-
-        zero = jnp.zeros((8, rows), F32)
-        z, delta = lax.fori_loop(0, pieces, second, (zero, zero), unroll=True)
+            z = z + folded(e, jnp.sum)
+            delta = delta + folded(e * dp, jnp.sum)
         inv = 1.0 / jnp.sum(z, axis=0, keepdims=True)
         delta = jnp.sum(delta, axis=0, keepdims=True) * inv
-
-        def terms(j):
-            at = pl.ds(pl.multiple_of(j * piece, piece), piece)
-            prob = sbuf[at, :] * inv
-            prob_b = prob.astype(BF16)
-            ds = (prob * (dbuf[at, :] - delta) * scale).astype(BF16)
-            pbuf[at, :] = prob_b
-            dsbuf[at, :] = ds
-            grad_k = jnp.dot(ds, q, preferred_element_type=F32)
-            grad_v = jnp.dot(prob_b, g, preferred_element_type=F32)
-            return at, grad_k, grad_v
-
-        def third(j, carry):
-            at, grad_k, grad_v = terms(j)
-            grads[h, 0, at, :] = grad_k.astype(BF16)
-            grads[h, 1, at, :] = grad_v.astype(BF16)
-            return carry
-
-        lax.fori_loop(0, pieces - 1, third, 0, unroll=True)
-        _, grad_k, grad_v = terms(pieces - 1)
-        sc_all[h, 0] = grad_k[:tokens]
-        sc_all[h, 1] = grad_v[:tokens]
+        inv_scale = inv * scale
+        q = q_ref[:, cols]
+        g = glive[:, cols]
+        for start, size in pieces:
+            at = slice(start, start + size)
+            e = sbuf[at, :]
+            pbuf[at, :] = (e * inv).astype(BF16)
+            dsbuf[at, :] = (e * inv_scale * (dbuf[at, :] - delta)).astype(BF16)
+        for start in range(0, base, 2 * rows):
+            at = slice(start, start + 2 * rows)
+            grads[h, 0, at, :] = jnp.dot(
+                dsbuf[at, :], q, preferred_element_type=F32
+            ).astype(BF16)
+            grads[h, 1, at, :] = jnp.dot(
+                pbuf[at, :], g, preferred_element_type=F32
+            ).astype(BF16)
+        at = slice(base, base + tokens)
+        sc_all[h, 0] = jnp.dot(dsbuf[at, :], q, preferred_element_type=F32)
+        sc_all[h, 1] = jnp.dot(pbuf[at, :], g, preferred_element_type=F32)
+        for k in range(4):
+            rs(h, k).start()
         out = jnp.dot(vt[...], pbuf[...], preferred_element_type=F32)
         att_ref[:, cols] = jnp.where(live_lane, out, 0.0).T.astype(BF16)
         gq = jnp.dot(kt[...], dsbuf[...], preferred_element_type=F32)
@@ -502,8 +499,6 @@
             for k in (2, 5, 6, 7):
                 ag(h, k, False).wait_recv()
             attend(h)
-            for k in range(4):
-                rs(h, k).start()
 
         @pl.when(t >= 5)
         def _():
@@ -575,16 +570,20 @@
         scene_sum(k).wait_send()
 
 
-def finish_kernel(heads, n_head, a_ref, b_ref, c_ref, d_ref, sg_ref, ao, bo, co, do, sko, svo):
-    ao[...] = a_ref[...]
-    bo[...] = b_ref[...]
-    co[...] = c_ref[...]
-    do[...] = d_ref[...]
+def finish_kernel(
+    heads, n_head, a_ref, b_ref, c_ref, d_ref, sg_ref, ao, bo, co, do, sko, svo, sems
+):
+    pairs = ((a_ref, ao), (b_ref, bo), (c_ref, co), (d_ref, do))
+    moves = [pltpu.make_async_copy(x, y, sems.at[i]) for i, (x, y) in enumerate(pairs)]
+    for move in moves:
+        move.start()
     for t in range(n_head):
         for h in range(heads):
             at = (t * heads + h) * DH
             sko[:, at:at + DH] = sg_ref[t, h:h + 1, :].astype(BF16)
             svo[:, at:at + DH] = sg_ref[t, 8 + h:9 + h, :].astype(BF16)
+    for move in moves:
+        move.wait()
 
 
 def fused_device(queries, keys, values, grad_out, scene_keys, scene_values, valid, pattern):
@@ -598,6 +597,7 @@
     tokens = 8 * n_head
     flat = 2 * heads * n_head
     vmem = pl.BlockSpec(memory_space=pltpu.VMEM)
+    anywhere = pl.BlockSpec(memory_space=pl.ANY)
     smem = pl.BlockSpec(memory_space=pltpu.SMEM)
     wide = jax.ShapeDtypeStruct((rows, features), BF16)
     dma = pltpu.SemaphoreType.DMA
@@ -620,6 +620,8 @@
             pltpu.VMEM((DH, total), BF16),
             pltpu.VMEM((DH, total), BF16),
             pltpu.VMEM((rows, features), BF16),
+            pltpu.VMEM((heads, DH, rows), BF16),
+            pltpu.VMEM((heads, DH, rows), BF16),
             pltpu.VMEM((n_head, 16, DH), F32),
             pltpu.VMEM((n_head, 16, DH), F32),
             pltpu.VMEM((n_head, 16, DH), F32),
@@ -642,8 +644,9 @@
         pl.pallas_call(
             functools.partial(finish_kernel, heads, n_head),
             out_shape=[wide] * 4 + [row] * 2,
-            in_specs=[vmem] * 5,
-            out_specs=[vmem] * 6,
+            in_specs=[anywhere] * 4 + [vmem],
+            out_specs=[anywhere] * 4 + [vmem] * 2,
+            scratch_shapes=[dma((4,))],
         )(*out)
     )
 

time: 80.6 us -> 127 us (1.58)
  Pallas kernels: 74.5 us -> 121 us
    pallas_call x1, Pallas kernels: 2.52 us -> 50.1 us  [fused_device(): pl.pallas_call(functools.partial(finish_kernel, heads, n_head), out_shape...]
where the time goes in v3:
time: 127 us
  Pallas kernels  121 us (95%)
  local copies, waits for them, and re-layouts  5.11 us (4%)
    pallas_call x1, Pallas kernels, fused_device(): pl.pallas_call(functools.partial(fused_kernel, heads, n_head, blocks), ou...  71.1 us
    pallas_call x1, Pallas kernels, fused_device(): pl.pallas_call(functools.partial(finish_kernel, heads, n_head), out_shape...  50.1 us
    unnamed x17, local copies, waits for them, and re-layouts  5.11 us

profile of v3, /device:TPU:0, one launch (start us, length us, event | category | flops | bytes accessed | tf_op | source)
XLA Modules:
  0.0 127.0 jit_solution(9753767154607489195)
XLA Ops:
  0.6 0.0 copy-start.7
  0.6 0.0 copy-start.5
  0.7 0.8 copy.14.pattern_ref
  1.4 0.0 copy-done.7
  1.4 0.0 copy-done.5
  1.4 0.0 copy-start.6
  1.4 0.7 copy-done.6
  2.1 71.1 %shard_map.127 = (bf16[256,768]{1,0:T(8,128)(2,1)S(1)}, bf16[256,768]{1,0:T(8,128)(2,1)S(1)}, bf16[256,768]{1,0:T(8,128)(2,1)S(1)}, bf16[256,768]{1,0:T(8,128)(2,1)S(1)}, f32[4,16,128]{2,1,0:T(8,128)S(1)}) custom-call(s32[32]{0:T(128)S(1)} %copy-done.7, s32[32,3]{1,0:T(8,128)S(1)} %copy.14.pattern_ref, bf16[256,768]{1,0:T(8,128)(2,1)} %q_ref.1, ...), custom_call_target="tpu_custom_call" | custom-call | tf_op jit(solution)/shard_map/pallas_call | solution.py:604
  73.2 0.0 copy-start
  73.2 0.7 copy-done
  74.0 0.0 copy-start.1
  74.0 0.8 copy-done.1
  74.7 0.0 copy-start.2
  74.7 0.8 copy-done.2
  75.5 0.0 copy-start.3
  75.5 0.8 copy-done.3
  76.3 0.0 copy-start.4
  76.3 0.6 copy-done.4
  76.9 50.1 %shard_map.128 = (bf16[256,768]{1,0:T(8,128)(2,1)}, bf16[256,768]{1,0:T(8,128)(2,1)}, bf16[256,768]{1,0:T(8,128)(2,1)}, bf16[256,768]{1,0:T(8,128)(2,1)}, bf16[1...) custom-call(bf16[256,768]{1,0:T(8,128)(2,1)} %copy-done, bf16[256,768]{1,0:T(8,128)(2,1)} %copy-done.1, ...), custom_call_target="tpu_custom_call" | custom-call | tf_op jit(solution)/shard_map/pallas_call | solution.py:644
Async XLA Ops:
  0.6 0.8 copy-start.7
  0.6 0.8 copy-start.5
  1.4 0.7 copy-start.6
  73.2 0.7 copy-start
  74.0 0.8 copy-start.1
  74.7 0.8 copy-start.2
  75.5 0.8 copy-start.3
  76.3 0.6 copy-start.4

commit v4 on v3

--- a/solution.py
+++ b/solution.py
@@ -570,22 +570,6 @@
         scene_sum(k).wait_send()
 
 
-def finish_kernel(
-    heads, n_head, a_ref, b_ref, c_ref, d_ref, sg_ref, ao, bo, co, do, sko, svo, sems
-):
-    pairs = ((a_ref, ao), (b_ref, bo), (c_ref, co), (d_ref, do))
-    moves = [pltpu.make_async_copy(x, y, sems.at[i]) for i, (x, y) in enumerate(pairs)]
-    for move in moves:
-        move.start()
-    for t in range(n_head):
-        for h in range(heads):
-            at = (t * heads + h) * DH
-            sko[:, at:at + DH] = sg_ref[t, h:h + 1, :].astype(BF16)
-            svo[:, at:at + DH] = sg_ref[t, 8 + h:9 + h, :].astype(BF16)
-    for move in moves:
-        move.wait()
-
-
 def fused_device(queries, keys, values, grad_out, scene_keys, scene_values, valid, pattern):
     n_head = lax.axis_size("head")
     rows, features = queries.shape
@@ -597,7 +581,6 @@
     tokens = 8 * n_head
     flat = 2 * heads * n_head
     vmem = pl.BlockSpec(memory_space=pltpu.VMEM)
-    anywhere = pl.BlockSpec(memory_space=pl.ANY)
     smem = pl.BlockSpec(memory_space=pltpu.SMEM)
     wide = jax.ShapeDtypeStruct((rows, features), BF16)
     dma = pltpu.SemaphoreType.DMA
@@ -639,16 +622,10 @@
             collective_id=0, has_side_effects=True, vmem_limit_bytes=52 * 1024 * 1024
         ),
     )(valid, pattern, queries, keys, values, grad_out, scene_keys, scene_values)
-    row = jax.ShapeDtypeStruct((1, n_head * features), BF16)
-    return tuple(
-        pl.pallas_call(
-            functools.partial(finish_kernel, heads, n_head),
-            out_shape=[wide] * 4 + [row] * 2,
-            in_specs=[anywhere] * 4 + [vmem],
-            out_specs=[anywhere] * 4 + [vmem] * 2,
-            scratch_shapes=[dma((4,))],
-        )(*out)
-    )
+    att, gq, gk, gv, sg = out
+    gsk = sg[:, :heads].reshape(1, n_head * features).astype(BF16)
+    gsv = sg[:, 8:8 + heads].reshape(1, n_head * features).astype(BF16)
+    return att, gq, gk, gv, gsk, gsv
 
 
 def solution(mesh):

time: 127 us -> 77.7 us (0.61)
  Pallas kernels: 121 us -> 71.1 us
    pallas_call x1 -> x0, Pallas kernels: 50.1 us -> none  [fused_device(): pl.pallas_call(functools.partial(finish_kernel, heads, n_head), out_shape...]
    unnamed x17 -> x11, local copies, waits for them, and re-layouts: 5.11 us -> 4.47 us
where the time goes in v4:
time: 77.7 us; the launch traced here: 77.5 us
  Pallas kernels  71.1 us (92%)
  local copies, waits for them, and re-layouts  5.7 us (7%)
    pallas_call x1, Pallas kernels, fused_device(): pl.pallas_call(functools.partial(fused_kernel, heads, n_head, blocks), ou...  71.1 us
    unnamed x11, local copies, waits for them, and re-layouts  4.47 us

profile of v4, /device:TPU:0, one launch (start us, length us, event | category | flops | bytes accessed | tf_op | source)
XLA Modules:
  0.0 77.5 jit_solution(13372774099496679100)
XLA Ops:
  0.6 0.0 copy-start
  0.6 0.0 copy-start.2
  0.7 0.8 copy.15.pattern_ref
  1.4 0.0 copy-done
  1.4 0.0 copy-done.2
  1.4 0.0 copy-start.1
  1.4 0.7 copy-done.1
  2.1 71.1 %shard_map.127 = (bf16[256,768]{1,0:T(8,128)(2,1)S(1)}, bf16[256,768]{1,0:T(8,128)(2,1)S(1)}, bf16[256,768]{1,0:T(8,128)(2,1)S(1)}, bf16[256,768]{1,0:T(8,128)(2,1)S(1)}, f32[4,16,128]{2,1,0:T(8,128)S(1)}) custom-call(s32[32]{0:T(128)S(1)} %copy-done.2, s32[32,3]{1,0:T(8,128)S(1)} %copy.15.pattern_ref, bf16[256,768]{1,0:T(8,128)(2,1)} %q_ref.1, ...), custom_call_target="tpu_custom_call" | custom-call | tf_op jit(solution)/shard_map/pallas_call | solution.py:587
  73.3 0.6 convert_element_type.24
  73.9 0.6 convert_element_type.25
  74.5 0.7 copy.20
  75.2 0.7 copy.21
  76.0 0.7 copy.22
  76.7 0.7 copy.23
  (2 shorter events, 0.0 us)
Async XLA Ops:
  0.6 0.8 %copy-start = (bf16[1,3072]{1,0:T(2,128)(2,1)S(1)}, bf16[1,3072]{1,0:T(2,128)(2,1)}, u32[]{:S(2)}) copy-start(bf16[1,3072]{1,0:T(2,128)(2,1)} %sk_ref.1) | copy-start | bytes 18436
  0.6 0.8 %copy-start.2 = (s32[32]{0:T(128)S(1)}, s32[32]{0:T(128)}, u32[]{:S(2)}) copy-start(s32[32]{0:T(128)} %valid_ref.1) | copy-start | bytes 388
  1.4 0.7 copy-start.1
